TPU v7x, 32 devices: a whole 2x2x4 slice. The times are simulated.
32 devices in a mesh: dp: 8 (over z, y), ctx: 4 (over x, core).
Axes of the slice: x: 2, y: 2, z: 4, core: 2. Of those that a mesh axis runs over, the one named last changes fastest.
Arguments:
- queries_q: bfloat16 [8, 512, 1792], P('dp', 'ctx'), may hold values from -5 to 5
- keys: bfloat16 [8, 512, 256], P('dp', 'ctx'), may hold values from -5 to 5
- values: bfloat16 [8, 512, 256], P('dp', 'ctx'), may hold values from -6 to 6
- lengths: int32 [8, 4], P('dp'), may hold values from 1 to 384, 512 in all within a row
- query_emb: bfloat16 [1024, 1792], P('dp'), may hold values from -6 to 6
- positive: int32 [1024], P('dp'), may hold values from 0 to 31
Outputs:
- query_grad: float32 [1024, 1792], P('dp')
- grad_queries: bfloat16 [8, 512, 1792], P('dp', 'ctx')
- grad_keys: bfloat16 [8, 512, 256], P('dp', 'ctx')
- grad_values: bfloat16 [8, 512, 256], P('dp', 'ctx')
Inputs may be any that keep to these rules, and one draw needn't show every extreme that they name: The 4 lengths of each row sum to 512, and the longest is 384.
All inputs are finite; a program needn't handle non-finite values.
Results may differ from a plain program's by a relative error of at most 0.012.
The roundings to bfloat16 on the way count: a program that leaves them out, or rounds other values in their place, can miss the bound.
Values may be sent and summed in bfloat16 or wider, within the bound.
A program may use at most 64 MiB of HBM per device.

v0:
```python
import jax
import jax.numpy as jnp
from jax import lax
from jax.sharding import PartitionSpec as P

HEAD_DIM = 128
HEADS = 14
KV_HEADS = 2


INVERSE_TEMPER = 0.05
EPSILON = 1e-06
FULL_ACCURACY = lax.Precision.HIGHEST


def document_ids(lengths_row, positions):
    doc_ends = jnp.cumsum(lengths_row)
    return jnp.sum((positions[:, None] >= doc_ends[None, :]).astype(jnp.int32), axis=1)


def rescale_back(inverse, unit_vec, upstream):
    inner_sum = jnp.sum(unit_vec * upstream, axis=1, keepdims=True)
    return inverse * (upstream - unit_vec * inner_sum)


def predicted_less_label(similarity_logits, positive):
    exp_logits = jnp.exp(similarity_logits)
    target = (
        jnp.arange(similarity_logits.shape[1], dtype=jnp.int32)[None, :] == positive[:, None]
    ).astype(jnp.float32)
    return exp_logits / jnp.sum(exp_logits, axis=1, keepdims=True) - target


def per_device(queries_q, keys, values, lengths, query_emb, positive):
    tok_rows = queries_q.shape[1]
    emb_width = queries_q.shape[2]
    kv_width = keys.shape[2]
    per_group = HEADS // KV_HEADS
    factor = HEAD_DIM ** (-0.5)
    whole_keys, whole_values = (
        lax.all_gather(keys, "ctx", axis=1, tiled=True),
        lax.all_gather(values, "ctx", axis=1, tiled=True),
    )
    seq_len = whole_keys.shape[1]
    tile_of_lookups = min(512, seq_len)
    first_pos = lax.axis_index("ctx") * tok_rows
    key_pos = jnp.arange(seq_len, dtype=jnp.int32)
    query_pos = first_pos + jnp.arange(tok_rows, dtype=jnp.int32)
    len_row = lengths[0]
    key_doc = document_ids(len_row, key_pos)
    query_doc = document_ids(len_row, query_pos)
    doc_index = jnp.arange(len_row.shape[0], dtype=jnp.int32)
    doc_starts = jnp.cumsum(len_row) - len_row
    doc_begin = jnp.sum(jnp.where(doc_index == query_doc[0], doc_starts, 0))
    low_block = doc_begin // tile_of_lookups
    high_block = (first_pos + tok_rows - 1) // tile_of_lookups + 1
    q_heads = queries_q[0].reshape(tok_rows, KV_HEADS, per_group, HEAD_DIM)
    k_all = whole_keys[0].reshape(seq_len, KV_HEADS, HEAD_DIM)
    v_all = whole_values[0].reshape(seq_len, KV_HEADS, HEAD_DIM)

    def block_rows(block_idx, table):
        return lax.dynamic_slice_in_dim(table, block_idx * tile_of_lookups, tile_of_lookups, 0)

    def block_scores(block_idx):
        k_rows = block_rows(block_idx, k_all)
        doc_rows = block_rows(block_idx, key_doc)
        pos_rows = block_idx * tile_of_lookups + jnp.arange(tile_of_lookups, dtype=jnp.int32)
        raw_scores = (
            jnp.einsum("tgqd,sgd->gqts", q_heads, k_rows, preferred_element_type=jnp.float32)
            * factor
        )
        allowed = (query_doc[:, None] == doc_rows[None, :]) & (
            pos_rows[None, :] <= query_pos[:, None]
        )
        return jnp.where(allowed, raw_scores, -jnp.inf)

    def stat_step(block_idx, carry):
        row_top, row_total = carry
        scores = block_scores(block_idx)
        new_top = jnp.maximum(row_top, jnp.max(scores, axis=-1, keepdims=True))
        row_total = row_total * jnp.exp(row_top - new_top) + jnp.sum(
            jnp.exp(scores - new_top), axis=-1, keepdims=True
        )
        return (new_top, row_total)

    stat_shape = (KV_HEADS, per_group, tok_rows, 1)
    running_figures_start = (
        jnp.full(stat_shape, -1e30, jnp.float32),
        jnp.zeros(stat_shape, jnp.float32),
    )
    row_top, row_total = lax.fori_loop(low_block, high_block, stat_step, running_figures_start)
    log_total = row_top + jnp.log(row_total)

    def out_step(block_idx, out_acc):
        weights = jnp.exp(block_scores(block_idx) - log_total).astype(jnp.bfloat16)
        v_rows = block_rows(block_idx, v_all)
        return out_acc + jnp.einsum(
            "gqts,sgd->tgqd", weights, v_rows, preferred_element_type=jnp.float32
        )

    head_shape = (tok_rows, KV_HEADS, per_group, HEAD_DIM)
    attended = lax.fori_loop(
        low_block, high_block, out_step, jnp.zeros(head_shape, jnp.float32)
    ).reshape(tok_rows, emb_width)
    member = (doc_index[:, None] == query_doc[None, :]).astype(jnp.float32)
    doc_sum = lax.psum(jnp.dot(member, attended, precision=FULL_ACCURACY), "ctx")
    doc_len = len_row.astype(jnp.float32)[:, None]
    doc_emb = doc_sum / doc_len
    doc_inv = lax.rsqrt(jnp.sum(doc_emb * doc_emb, axis=1, keepdims=True) + EPSILON)
    document_normalized = doc_emb * doc_inv
    query_f = query_emb.astype(jnp.float32)
    query_inv = lax.rsqrt(jnp.sum(query_f * query_f, axis=1, keepdims=True) + EPSILON)
    query_normalized = query_f * query_inv
    every_document = lax.all_gather(document_normalized, "dp", axis=0, tiled=True)
    similarity_logits = (
        jnp.dot(query_normalized, every_document.T, precision=FULL_ACCURACY) / INVERSE_TEMPER
    )
    scaling_coefficient = predicted_less_label(similarity_logits, positive)
    query_upstream_gradient = (
        jnp.dot(scaling_coefficient, every_document, precision=FULL_ACCURACY) / INVERSE_TEMPER
    )
    passage_contributions = (
        jnp.dot(scaling_coefficient.T, query_normalized, precision=FULL_ACCURACY) / INVERSE_TEMPER
    )
    document_upstream_gradient = lax.psum_scatter(
        passage_contributions, "dp", scatter_dimension=0, tiled=True
    )
    query_grad = rescale_back(query_inv, query_normalized, query_upstream_gradient)
    passage_derivative = (
        rescale_back(doc_inv, document_normalized, document_upstream_gradient) / doc_len
    )
    out_grad = jnp.dot(member.T, passage_derivative, precision=FULL_ACCURACY)
    out_heads = out_grad.astype(jnp.bfloat16).reshape(head_shape)
    row_delta = jnp.sum((out_grad * attended).reshape(head_shape), axis=-1)
    row_delta = jnp.transpose(row_delta, (1, 2, 0))[..., None]

    def back_step(block_idx, carry):
        query_acc, key_terms, value_terms = carry
        probability = jnp.exp(block_scores(block_idx) - log_total)
        weights = probability.astype(jnp.bfloat16)
        k_rows = block_rows(block_idx, k_all)
        v_rows = block_rows(block_idx, v_all)
        flow_grad = jnp.einsum(
            "tgqd,sgd->gqts", out_heads, v_rows, preferred_element_type=jnp.float32
        )
        score_grad = (probability * (flow_grad - row_delta)).astype(jnp.bfloat16)
        query_acc = query_acc + jnp.einsum(
            "gqts,sgd->tgqd", score_grad, k_rows, preferred_element_type=jnp.float32
        )
        key_part = (
            jnp.einsum("gqts,tgqd->sgd", score_grad, q_heads, preferred_element_type=jnp.float32)
            * factor
        )
        value_part = jnp.einsum(
            "gqts,tgqd->sgd", weights, out_heads, preferred_element_type=jnp.float32
        )
        key_terms = lax.dynamic_update_slice_in_dim(
            key_terms, key_part, block_idx * tile_of_lookups, 0
        )
        value_terms = lax.dynamic_update_slice_in_dim(
            value_terms, value_part, block_idx * tile_of_lookups, 0
        )
        return (query_acc, key_terms, value_terms)

    term_shape = (seq_len, KV_HEADS, HEAD_DIM)
    back_init = (
        jnp.zeros(head_shape, jnp.float32),
        jnp.zeros(term_shape, jnp.float32),
        jnp.zeros(term_shape, jnp.float32),
    )
    query_acc, key_terms, value_terms = lax.fori_loop(low_block, high_block, back_step, back_init)
    grad_queries = (query_acc * factor).astype(jnp.bfloat16).reshape(1, tok_rows, emb_width)
    key_sum, value_sum = (
        lax.psum_scatter(
            key_terms.reshape(1, seq_len, kv_width).astype(jnp.bfloat16),
            "ctx",
            scatter_dimension=1,
            tiled=True,
        ).astype(jnp.float32),
        lax.psum_scatter(
            value_terms.reshape(1, seq_len, kv_width).astype(jnp.bfloat16),
            "ctx",
            scatter_dimension=1,
            tiled=True,
        ).astype(jnp.float32),
    )
    return (query_grad, grad_queries, key_sum.astype(jnp.bfloat16), value_sum.astype(jnp.bfloat16))


def solution(mesh):
    placed = (
        P("dp", "ctx", None),
        P("dp", "ctx", None),
        P("dp", "ctx", None),
        P("dp", None),
        P("dp", None),
        P("dp"),
    )
    return jax.shard_map(
        per_device,
        mesh=mesh,
        in_specs=placed,
        out_specs=(P("dp", None), P("dp", "ctx", None), P("dp", "ctx", None), P("dp", "ctx", None)),
        check_vma=False,
    )
```

profile of v0, /device:TPU:0, one launch (start us, length us, event | category | flops | bytes accessed | tf_op | source)
XLA Modules:
  0.0 219.4 jit_solution(10365522354407552835)
XLA Ops:
  7.2 0.8 reduce-window.8
  8.1 0.1 convert_reduce_fusion.1
  8.1 1.3 fusion.64
  12.1 0.1 convert_reduce_fusion
  12.2 0.7 bitcast_convert_fusion
  12.8 1.3 copy.64
  14.1 0.3 copy.69
  14.4 1.0 copy.63
  15.3 7.2 %all_gather.9 = bf16[1,512,256]{1,2,0:T(8,128)(2,1)S(1)} all-gather(bf16[1,128,256]{1,2,0:T(8,128)(2,1)S(1)} %copy.63), channel_id=1, replica_groups=mesh['dp'=8,'ctx'=4] {'ctx'}, dimensions={1}, use_global_device_ids=true | all-gather | bytes 327680 | tf_op jit(solution)/shard_map/all_gather | solution.py:41
  22.5 0.2 copy.68
  22.7 1.7 while.39
  22.8 0.2 compare_and_fusion.6
  23.0 0.7 fusion.101
  23.7 0.7 exponential_reduce_fusion.2
  24.5 0.1 copy.67
  24.6 5.9 %all_gather.10 = bf16[1,512,256]{1,2,0:T(8,128)(2,1)S(1)} all-gather(bf16[1,128,256]{1,2,0:T(8,128)(2,1)S(1)} %copy.67), channel_id=1, replica_groups=mesh['dp'=8,'ctx'=4] {'ctx'}, dimensions={1}, use_global_device_ids=true | all-gather | bytes 327680 | tf_op jit(solution)/shard_map/all_gather | solution.py:42
  30.5 0.2 copy.70
  30.7 0.1 broadcast.74.clone
  30.8 2.0 while.40
  30.8 0.2 compare_and_fusion.7
  31.0 1.7 fusion.105
  32.8 0.3 copy.71
  33.1 0.3 copy-done.6
  33.4 0.5 fusion.61
  33.9 11.6 %psum.7 = f32[4,1792]{1,0:T(4,128)S(1)} all-reduce(f32[4,1792]{1,0:T(4,128)S(1)} %fusion.61), channel_id=1, replica_groups=mesh['dp'=8,'ctx'=4] {'ctx'}, use_global_device_ids=true, to_apply=%region_11.12 | all-reduce | flops 7168 | bytes 57344 | tf_op jit(solution)/shard_map/psum | solution.py:106
  45.6 0.2 multiply_reduce_fusion.1
  45.8 0.1 multiply_bitcast_fusion
  45.8 31.0 %all-gather = f32[8,4,1792]{2,1,0:T(4,128)S(1)} all-gather(f32[1,4,1792]{2,1,0:T(4,128)S(1)} %multiply_bitcast_fusion), channel_id=1, replica_groups=mesh['dp'=8,'ctx'=4] {'dp'}, dimensions={0}, use_global_device_ids=true | all-gather | bytes 258048 | tf_op jit(solution)/shard_map/all_gather | solution.py:114
  76.9 0.1 reshape.126
  77.0 0.2 fusion.48
  77.1 1.1 fusion.67
  78.2 2.1 convolution_multiply_fusion.1
  80.3 0.0 reduce-scatter.3.cloned.1.call-start
  80.4 0.3 copy.73
  80.7 1.2 dynamic-slice
  82.6 68.3 %all-reduce.3.cloned.1.call-done = f32[32,1792]{1,0:T(8,128)} async-done(((f32[32,1792]{1,0:T(8,128)}), f32[32,1792]{1,0:T(8,128)}) %all-reduce.3.cloned.1.call-update) | async-done | bytes 229392
  150.9 1.0 multiply_reduce_fusion
  151.9 2.2 fusion.66
  154.1 0.3 copy.74
  154.4 1.3 copy.72
  155.7 1.0 copy.78
  156.7 0.1 reduce_sum.98
  156.7 0.1 broadcast.74
  156.8 0.7 broadcast.76
  157.5 0.7 broadcast.76.clone
  158.2 9.9 %while.41 = (s32[]{:T(128)}, f32[128,2,7,128]{3,0,2,1:T(8,128)S(1)}, bf16[512,2,128]{2,0,1:T(8,128)(2,1)}, bf16[512,2,128]{2,0,1:T(8,128)(2,1)}, s32[]{:T(128)},...) while((s32[]{:T(128)}, ...), condition=%wide.region_19.20_spmd.clone, body=%wide.region_18.19_spmd.clone.sunk | while | flops 1184268928 | bytes 38265596 | solution.py:171
  158.2 2.4 %fusion.116 = f32[2,512,128,7]{2,1,3,0:T(8,128)} fusion(bf16[128,2,7,128]{3,0,2,1:T(8,128)(2,1)S(1)} %get-tuple-element.786, bf16[512,2,128]{2,0,1:T(8,128)(2,1)S(1)} %get-tuple-element.785), kind=kOutput, calls=%fused_computation.44.clone.1 | convolution fusion | flops 234881024 | bytes 4390912 | tf_op jit(solution)/shard_map/while/body/tgqd,sgd->gqts/dot_general | solution.py:69
  160.7 0.2 compare_and_fusion.8
  160.9 3.2 %fusion.117 = bf16[2,7,128,512]{2,3,1,0:T(8,128)(2,1)S(1)} fusion(f32[2,512,128,7]{2,1,3,0:T(8,128)} %fusion.116, bf16[128,2,7,128]{3,0,2,1:T(8,128)(2,1)S(1)} %copy-done.2, f32[2,7,128]{2,1,0:T(8,128)S(1)} %bitcast.206, f32[2,7,128]{2,1,0:T(8,128)S(1)} %bitcast.208, pred[128,512]{0,1:T(8,128)(4,1)S(1)} %compare_and_fusion.8, ...), kind=kOutput, calls=%fused_computation.29.clone.1 | convolution fusion | flops 240386048 | bytes 6305792 | tf_op jit(solution)/shard_map/while/body/tgqd,sgd->gqts/dot_general | solution.py:143
  164.1 1.1 fusion.118
  165.3 1.3 fusion.119
  166.6 1.6 fusion.120
  168.2 1.2 copy.80
  169.4 0.9 convert_element_type.75
  170.3 0.0 reduce-scatter.5.cloned.1.call-start
  170.4 1.7 fusion.45
  172.1 1.2 copy.81
  173.3 0.9 convert_element_type.77
  174.2 1.2 fusion.47
  175.4 0.3 copy.79
  175.7 0.1 multiply_convert_fusion
  175.8 1.0 copy.82
  176.8 12.9 %reduce-scatter.3.cloned.1.call-done = bf16[1,128,256]{2,1,0:T(8,128)(2,1)} async-done(((bf16[1,512,256]{2,1,0:T(8,128)(2,1)}), bf16[1,128,256]{2,1,0:T(8,128)(2,1)}) %reduce-scatter.3.cloned.1.call-update) | async-done | bytes 65552 | tf_op jit(solution)/shard_map/reduce_scatter | solution.py:174
  189.7 23.1 %reduce-scatter.5.cloned.1.call-done = bf16[1,128,256]{2,1,0:T(8,128)(2,1)} async-done(((bf16[1,512,256]{2,1,0:T(8,128)(2,1)}), bf16[1,128,256]{2,1,0:T(8,128)(2,1)}) %reduce-scatter.5.cloned.1.call-update) | async-done | bytes 65552 | tf_op jit(solution)/shard_map/reduce_scatter | solution.py:180
  (40 shorter events, 0.2 us)
Async XLA Ops:
  7.2 143.7 %all-reduce.3.cloned.1.call-start = ((), (), s32[]{:S(2)}) async-start(), calls=%async_computation.4 | async-start | bytes 458752
  12.8 32.7 %copy-start.10 = (f32[4]{0:T(128)}, f32[4]{0:T(128)S(1)}, u32[]{:S(2)}) copy-start(f32[4]{0:T(128)S(1)} %bitcast_convert_fusion) | copy-start | bytes 52
  22.7 1.7 copy-start.5
  32.8 0.6 copy-start.6
  32.8 44.2 %copy-start.1 = (bf16[128,1792]{1,0:T(8,128)(2,1)S(1)}, bf16[128,1792]{1,0:T(8,128)(2,1)}, u32[]{:S(2)}) copy-start(bf16[128,1792]{1,0:T(8,128)(2,1)} %param.16) | copy-start | bytes 1376260
  78.2 2.1 copy-start.3
  78.2 77.5 %copy-start.8 = (f32[128]{0:T(128)}, f32[128]{0:T(128)S(1)}, u32[]{:S(2)}) copy-start(f32[128]{0:T(128)S(1)} %get-tuple-element.468) | copy-start | bytes 1540
  80.3 109.4 %reduce-scatter.3.cloned.1.call-start = ((), (), s32[]{:S(2)}) async-start(), calls=%async_computation.2 | async-start | bytes 327680 | tf_op jit(solution)/shard_map/reduce_scatter | solution.py:174
  158.2 12.1 %copy-start.4 = (f32[128,32]{0,1:T(8,128)S(1)}, f32[128,32]{0,1:T(8,128)}, u32[]{:S(2)}) copy-start(f32[128,32]{0,1:T(8,128)} %copy-done.3) | copy-start | bytes 49156
  158.2 12.1 %copy-start.9 = (f32[128]{0:T(128)S(1)}, f32[128]{0:T(128)}, u32[]{:S(2)}) copy-start(f32[128]{0:T(128)} %copy-done.8) | copy-start | bytes 1540
  158.2 2.7 %copy-start.2 = (bf16[128,2,7,128]{3,0,2,1:T(8,128)(2,1)S(1)}, bf16[128,2,7,128]{3,0,2,1:T(8,128)(2,1)}, u32[]{:S(2)}) copy-start(bf16[128,2,7,128]{3,0,2,1:T(8,128)(2,1)} %get-tuple-element.789) | copy-start | bytes 1376260 | tf_op jit(solution)/shard_map/while
  158.2 2.7 %copy-start.7 = (f32[2,7,128,1]{2,1,0,3:T(8,128)S(1)}, f32[2,7,128,1]{2,1,0,3:T(8,128)}, u32[]{:S(2)}) copy-start(f32[2,7,128,1]{2,1,0,3:T(8,128)} %get-tuple-element.787) | copy-start | bytes 21508 | tf_op jit(solution)/shard_map/while
  164.1 2.5 %copy-start = (f32[2,512,128,7]{2,1,3,0:T(8,128)S(1)}, f32[2,512,128,7]{2,1,3,0:T(8,128)}, u32[]{:S(2)}) copy-start(f32[2,512,128,7]{2,1,3,0:T(8,128)} %fusion.116) | copy-start | bytes 11010052 | tf_op jit(solution)/shard_map/while
  170.3 42.5 %reduce-scatter.5.cloned.1.call-start = ((), (), s32[]{:S(2)}) async-start(), calls=%async_computation.3 | async-start | bytes 327680 | tf_op jit(solution)/shard_map/reduce_scatter | solution.py:180
Sparse Core Ops, SparseCore 0:
  80.4 70.4 all-reduce.2
  170.4 19.2 reduce-scatter.2
  192.7 20.0 reduce-scatter.4
where the time goes:
time: 220 us; the launch traced here: 219 us
  waiting for transfers between devices  104 us (47%)
  blocking collectives  55.8 us (25%)
  matrix products  19.6 us (9%)
  between operations  17.3 us (8%)
  local copies, waits for them, and re-layouts  14.8 us (7%)
  other arithmetic  7.26 us (3%)
    unnamed x4, waiting for transfers between devices  68.4 us
    all_gather x1, blocking collectives, per_device(): lax.all_gather(document_normalized, 'dp', axis=0, tiled=True)  31 us
    reduce_scatter x1, waiting for transfers between devices, per_device(): lax.psum_scatter(value_terms.reshape(1, seq_len, kv_width).astype(jnp.bfl...  23.1 us
    reduce_scatter x1, waiting for transfers between devices, per_device(): lax.psum_scatter(key_terms.reshape(1, seq_len, kv_width).astype(jnp.bfloa...  12.9 us
    psum x1, blocking collectives, per_device(): lax.psum(jnp.dot(member, attended, precision=FULL_ACCURACY), 'ctx')  11.6 us
    all_gather x1, blocking collectives, per_device(): lax.all_gather(keys, 'ctx', axis=1, tiled=True)  7.21 us
    unnamed x26, local copies, waits for them, and re-layouts  6.54 us
    all_gather x1, blocking collectives, per_device(): lax.all_gather(values, 'ctx', axis=1, tiled=True)  5.9 us
  transfers between devices with their start and end apart: 3, of which 3 were waited for; matrix products, arithmetic and copies ran while one was open for 4% of the time, Pallas kernels for 0%

commit v1 on v0

v1 whole, which is shorter than its diff:
```python
import functools

import jax
import jax.numpy as jnp
from jax import lax
from jax.experimental import pallas as pl
from jax.experimental.pallas import tpu as pltpu
from jax.sharding import PartitionSpec as P

HEAD_DIM = 128
HEADS = 14
KV_HEADS = 2
PER_GROUP = HEADS // KV_HEADS
DOCS = 4
WIRE = KV_HEADS * DOCS

SCALE_UP = 20.0
EPSILON = 1e-06
NEG = -1e30
F32 = jnp.float32
BF16 = jnp.bfloat16
MESH = pl.DeviceIdType.MESH


def dot_nn(a, b):
    return lax.dot_general(a, b, (((1,), (0,)), ((), ())), preferred_element_type=F32)


def dot_nt(a, b):
    return lax.dot_general(a, b, (((1,), (1,)), ((), ())), preferred_element_type=F32)


def dot_tn(a, b):
    return lax.dot_general(a, b, (((0,), (0,)), ((), ())), preferred_element_type=F32)


def split(x):
    high = x.astype(BF16)
    return high, (x - high.astype(F32)).astype(BF16)


def swap_halves(x):
    return jnp.concatenate([x[DOCS:], x[:DOCS]], axis=0)


def doc_row_sum(x):
    rows = jnp.sum(x, axis=1, keepdims=True)
    return rows + swap_halves(rows)


def kernel(
    n_ctx, n_dp,
    len_ref, q_ref, k_ref, v_ref, emb_ref, pos_ref,
    qg_ref, gq_ref, gk_ref, gv_ref,
    k_all, v_all, q_s, probs, att, bias, sums, units, terms, doc_hi, doc_lo,
    doc_grad, out_low, s_grad, weights, k_out, v_out, k_in, v_in,
    kv_send, kv_recv, sum_send, sum_recv, unit_send, unit_recv, term_send, term_recv,
    part_send, part_recv,
):
    me = lax.axis_index("ctx")
    row = lax.axis_index("dp")
    tok = q_ref.shape[1]
    seq = k_all.shape[0]
    emb = q_ref.shape[2]
    half = emb // 2
    factor = HEAD_DIM ** (-0.5)
    sibling = me + 1 - 2 * lax.rem(me, 2)

    def ctx_peer(t):
        return lax.rem(me + t, n_ctx)

    def dp_peer(t):
        return lax.rem(row + t, n_dp)

    def block(ref, idx):
        return ref.at[pl.ds(pl.multiple_of(idx * tok, tok), tok)]

    barrier = pltpu.get_barrier_semaphore()
    for t in range(1, n_ctx):
        pl.semaphore_signal(barrier, inc=1, device_id={"ctx": ctx_peer(t)}, device_id_type=MESH)
    for t in range(1, n_dp):
        pl.semaphore_signal(barrier, inc=1, device_id={"dp": dp_peer(t)}, device_id_type=MESH)
    pl.semaphore_wait(barrier, n_ctx + n_dp - 2)

    started = []

    def send(src, dst, send_sem, recv_sem, device):
        copy = pltpu.make_async_remote_copy(
            src_ref=src, dst_ref=dst, send_sem=send_sem, recv_sem=recv_sem,
            device_id=device, device_id_type=MESH,
        )
        copy.start()
        started.append(copy)

    def arrive(dst, send_sem, recv_sem, device):
        pltpu.make_async_remote_copy(
            src_ref=dst, dst_ref=dst, send_sem=send_sem, recv_sem=recv_sem,
            device_id=device, device_id_type=MESH,
        ).wait_recv()

    pairs = ((0, k_ref.at[0], k_all), (1, v_ref.at[0], v_all))
    n_half = n_ctx // 2
    for a, src, dst in pairs:
        for t in range(1, n_half):
            send(src, block(dst, me), kv_send.at[a, t], kv_recv.at[a, me], {"ctx": ctx_peer(2 * t)})
    for a, src, dst in pairs:
        send(src, block(dst, me), kv_send.at[a, 0], kv_recv.at[a, me], {"ctx": sibling})
    k_all[pl.ds(pl.multiple_of(me * tok, tok), tok), :] = k_ref[0]
    v_all[pl.ds(pl.multiple_of(me * tok, tok), tok), :] = v_ref[0]

    ends = []
    end = 0
    for d in range(DOCS):
        end = end + len_ref[0, d]
        ends.append(end)

    def doc_at(pos):
        doc = jnp.zeros(pos.shape, jnp.int32)
        for d in range(DOCS):
            doc = doc + (pos >= ends[d]).astype(jnp.int32)
        return doc

    first = me * tok
    q_pos = first + lax.broadcasted_iota(jnp.int32, (tok, seq), 0)
    k_pos = lax.broadcasted_iota(jnp.int32, (tok, seq), 1)
    allowed = (doc_at(q_pos) == doc_at(k_pos)) & (k_pos <= q_pos)
    bias[...] = jnp.where(allowed, 0.0, NEG)
    doc_col = doc_at(first + lax.broadcasted_iota(jnp.int32, (tok, HEAD_DIM), 0))
    wire_doc = lax.rem(lax.broadcasted_iota(jnp.int32, (WIRE, tok), 0), DOCS)
    member = (
        doc_at(first + lax.broadcasted_iota(jnp.int32, (WIRE, tok), 1)) == wire_doc
    ).astype(F32).astype(BF16)
    len_doc = lax.rem(lax.broadcasted_iota(jnp.int32, (WIRE, 1), 0), DOCS)
    doc_len = jnp.zeros((WIRE, 1), F32)
    for d in range(DOCS):
        doc_len = jnp.where(len_doc == d, len_ref[0, d].astype(F32), doc_len)
    for h in range(HEADS):
        q_s[h * tok:(h + 1) * tok, :] = q_ref[0, :, h * HEAD_DIM:(h + 1) * HEAD_DIM]
    q_sq = jnp.zeros((emb_ref.shape[0], HEAD_DIM), F32)
    for h in range(HEADS):
        part = emb_ref[:, h * HEAD_DIM:(h + 1) * HEAD_DIM].astype(F32)
        q_sq = q_sq + part * part
    q_inv = lax.rsqrt(jnp.sum(q_sq, axis=1, keepdims=True) + EPSILON)

    for a, src, dst in pairs:
        for t in range(1, n_half):
            idx = ctx_peer(2 * t)
            arrive(block(dst, idx), kv_send.at[a, t], kv_recv.at[a, idx], {"ctx": sibling})
            send(block(dst, idx), block(dst, idx), kv_send.at[a, n_half + t], kv_recv.at[a, idx],
                 {"ctx": sibling})
    for a, src, dst in pairs:
        for t in range(n_half):
            idx = lax.rem(sibling + 2 * t, n_ctx)
            arrive(block(dst, idx), kv_send.at[a, 0], kv_recv.at[a, idx], {"ctx": sibling})

    low_rows = lax.broadcasted_iota(jnp.int32, (WIRE, HEAD_DIM), 0) < DOCS

    def head_rows(g, i):
        return pl.ds(pl.multiple_of((g * PER_GROUP + i) * tok, tok), tok)

    def forward(i, carry):
        docs = []
        for g in range(KV_HEADS):
            rows = head_rows(g, i)
            k_g = k_all[:, g * HEAD_DIM:(g + 1) * HEAD_DIM]
            v_g = v_all[:, g * HEAD_DIM:(g + 1) * HEAD_DIM]
            scores = dot_nt(q_s[rows, :], k_g) * factor + bias[...]
            e = jnp.exp(scores - jnp.max(scores, axis=1, keepdims=True))
            p = e * (1.0 / jnp.sum(e, axis=1, keepdims=True))
            probs[rows, :] = p
            out = dot_nn(p.astype(BF16), v_g)
            att[rows, :] = out
            high, low = split(out)
            docs.append(dot_nn(member, high) + dot_nn(member, low))
        cols = pl.ds(pl.multiple_of(i * HEAD_DIM, HEAD_DIM), HEAD_DIM)
        sums[me, :, cols] = jnp.where(low_rows, docs[0], docs[1])
        return carry

    lax.fori_loop(0, PER_GROUP, forward, 0)
    for t in range(1, n_ctx):
        send(sums.at[me], sums.at[me], sum_send.at[t], sum_recv.at[me], {"ctx": ctx_peer(t)})
    for t in range(1, n_ctx):
        idx = ctx_peer(t)
        arrive(sums.at[idx], sum_send.at[t], sum_recv.at[idx], {"ctx": idx})
    doc_sum = sums[0]
    for c in range(1, n_ctx):
        doc_sum = doc_sum + sums[c]
    doc_emb = doc_sum / doc_len
    doc_inv = lax.rsqrt(doc_row_sum(doc_emb * doc_emb) + EPSILON)
    doc_unit = doc_emb * doc_inv
    units[row] = doc_unit
    for t in range(1, n_dp):
        send(units.at[row], units.at[row], unit_send.at[t], unit_recv.at[row], {"dp": dp_peer(t)})
    for t in range(1, n_dp):
        idx = dp_peer(t)
        arrive(units.at[idx], unit_send.at[t], unit_recv.at[idx], {"dp": idx})

    low_half = lax.broadcasted_iota(jnp.int32, (WIRE, half), 0) < DOCS
    for r in range(0, n_dp, 2):
        lefts, rights = [], []
        for s in range(2):
            w = units[r + s]
            other = swap_halves(w)
            lefts.append(jnp.where(low_half, w, other))
            rights.append(jnp.where(low_half, other, w))
        for at, x in ((0, jnp.concatenate(lefts, 0)), (half, jnp.concatenate(rights, 0))):
            high, low = split(x)
            doc_hi[r * WIRE:(r + 2) * WIRE, at:at + half] = high
            doc_lo[r * WIRE:(r + 2) * WIRE, at:at + half] = low

    q_emb = emb_ref[...]
    logits = (dot_nt(q_emb, doc_hi[...]) + dot_nt(q_emb, doc_lo[...])) * (q_inv * SCALE_UP)
    column = lax.broadcasted_iota(jnp.int32, logits.shape, 1)
    once = lax.rem(column, WIRE) < DOCS
    doc_of = (column // WIRE) * DOCS + lax.rem(column, DOCS)
    e = jnp.exp(logits)
    target = (doc_of == pos_ref[...]).astype(F32)
    coef = e / jnp.sum(jnp.where(once, e, 0.0), axis=1, keepdims=True) - target

    c_hi, c_lo = split(coef * (q_inv * SCALE_UP))
    for at in (0, half):
        part = emb_ref[:, at:at + half]
        w = dot_tn(c_hi, part) + dot_tn(c_lo, part)
        for r in range(n_dp):
            rows = w[r * WIRE:(r + 1) * WIRE]
            if at == 0:
                terms[1, r] = rows
            else:
                terms[1, r] = jnp.where(low_half, terms[1, r], rows)
    for t in range(1, n_dp):
        idx = dp_peer(t)
        send(terms.at[1, idx], terms.at[0, row], term_send.at[t], term_recv.at[row], {"dp": idx})
    terms[0, row] = terms[1, row]

    coef_once = jnp.where(once, coef, 0.0)
    inner = jnp.sum(coef_once * logits, axis=1, keepdims=True) * q_inv
    c_hi, c_lo = split(coef_once * SCALE_UP)
    step = 2 * HEAD_DIM
    for at in range(0, emb, step):
        d_hi = doc_hi[:, at:at + step]
        u = dot_nn(c_hi, d_hi) + dot_nn(c_lo, d_hi) + dot_nn(c_hi, doc_lo[:, at:at + step])
        qg_ref[:, at:at + step] = q_inv * (u - emb_ref[:, at:at + step].astype(F32) * inner)

    for t in range(1, n_dp):
        idx = dp_peer(t)
        arrive(terms.at[0, idx], term_send.at[t], term_recv.at[idx], {"dp": idx})
    w = terms[0, 0]
    for r in range(1, n_dp):
        w = w + terms[0, r]
    doc_grad[...] = doc_inv * (w - doc_unit * doc_row_sum(doc_unit * w)) / doc_len

    def backward(i, carry):
        cols = pl.ds(pl.multiple_of(i * HEAD_DIM, HEAD_DIM), HEAD_DIM)
        for g in range(KV_HEADS):
            rows = head_rows(g, i)
            og = jnp.zeros((tok, HEAD_DIM), F32)
            grads = doc_grad[:, cols]
            for d in range(DOCS):
                og = jnp.where(doc_col == d, grads[g * DOCS + d:g * DOCS + d + 1], og)
            delta = jnp.sum(og * att[rows, :], axis=1, keepdims=True)
            low = og.astype(BF16)
            out_low[rows, :] = low
            flow = dot_nt(low, v_all[:, g * HEAD_DIM:(g + 1) * HEAD_DIM])
            p = probs[rows, :]
            weights[rows, :] = p.astype(BF16)
            s_grad[rows, :] = (p * (flow - delta)).astype(BF16)
        return carry

    lax.fori_loop(0, PER_GROUP, backward, 0)

    span = PER_GROUP * tok
    for a, lhs, rhs, out, into, scale in (
        (0, weights, out_low, v_out, v_in, 1.0),
        (1, s_grad, q_s, k_out, k_in, factor),
    ):
        for g in range(KV_HEADS):
            part = dot_tn(lhs[g * span:(g + 1) * span, :], rhs[g * span:(g + 1) * span, :])
            out[:, g * HEAD_DIM:(g + 1) * HEAD_DIM] = (part * scale).astype(BF16)
        for t in range(1, n_ctx):
            idx = ctx_peer(t)
            send(block(out, idx), into.at[me], part_send.at[a, t], part_recv.at[a, me], {"ctx": idx})
        into[me] = out[pl.ds(pl.multiple_of(me * tok, tok), tok), :]

    for g in range(KV_HEADS):
        k_g = k_all[:, g * HEAD_DIM:(g + 1) * HEAD_DIM]
        for i in range(PER_GROUP):
            h = g * PER_GROUP + i
            dq = dot_nn(s_grad[h * tok:(h + 1) * tok, :], k_g) * factor
            gq_ref[0, :, h * HEAD_DIM:(h + 1) * HEAD_DIM] = dq.astype(BF16)

    for a, into, res in ((0, v_in, gv_ref), (1, k_in, gk_ref)):
        for t in range(1, n_ctx):
            idx = ctx_peer(t)
            arrive(into.at[idx], part_send.at[a, t], part_recv.at[a, idx], {"ctx": idx})
        total = into[0].astype(F32)
        for c in range(1, n_ctx):
            total = total + into[c].astype(F32)
        res[0] = total.astype(BF16)

    for copy in started:
        copy.wait_send()


def per_device(n_ctx, n_dp, queries_q, keys, values, lengths, query_emb, positive):
    tok, emb = queries_q.shape[1:]
    kv_width = keys.shape[2]
    seq = tok * n_ctx
    nq = query_emb.shape[0]
    n_rows = HEADS * tok
    half = emb // 2
    vmem = pl.BlockSpec(memory_space=pltpu.VMEM)
    dma = pltpu.SemaphoreType.DMA
    return pl.pallas_call(
        functools.partial(kernel, n_ctx, n_dp),
        out_shape=(
            jax.ShapeDtypeStruct((nq, emb), F32),
            jax.ShapeDtypeStruct(queries_q.shape, BF16),
            jax.ShapeDtypeStruct(keys.shape, BF16),
            jax.ShapeDtypeStruct(values.shape, BF16),
        ),
        in_specs=[pl.BlockSpec(memory_space=pltpu.SMEM)] + [vmem] * 5,
        out_specs=(vmem,) * 4,
        scratch_shapes=[
            pltpu.VMEM((seq, kv_width), BF16),
            pltpu.VMEM((seq, kv_width), BF16),
            pltpu.VMEM((n_rows, HEAD_DIM), BF16),
            pltpu.VMEM((n_rows, seq), F32),
            pltpu.VMEM((n_rows, HEAD_DIM), F32),
            pltpu.VMEM((tok, seq), F32),
            pltpu.VMEM((n_ctx, WIRE, half), F32),
            pltpu.VMEM((n_dp, WIRE, half), F32),
            pltpu.VMEM((2, n_dp, WIRE, half), F32),
            pltpu.VMEM((n_dp * WIRE, emb), BF16),
            pltpu.VMEM((n_dp * WIRE, emb), BF16),
            pltpu.VMEM((WIRE, half), F32),
            pltpu.VMEM((n_rows, HEAD_DIM), BF16),
            pltpu.VMEM((n_rows, seq), BF16),
            pltpu.VMEM((n_rows, seq), BF16),
            pltpu.VMEM((seq, kv_width), BF16),
            pltpu.VMEM((seq, kv_width), BF16),
            pltpu.VMEM((n_ctx, tok, kv_width), BF16),
            pltpu.VMEM((n_ctx, tok, kv_width), BF16),
            dma((2, n_ctx)), dma((2, n_ctx)),
            dma((n_ctx,)), dma((n_ctx,)),
            dma((n_dp,)), dma((n_dp,)),
            dma((n_dp,)), dma((n_dp,)),
            dma((2, n_ctx)), dma((2, n_ctx)),
        ],
        compiler_params=pltpu.CompilerParams(
            collective_id=0, has_side_effects=True, vmem_limit_bytes=56 * 1024 * 1024
        ),
    )(lengths, queries_q, keys, values, query_emb, positive[:, None])


def solution(mesh):
    placed = (
        P("dp", "ctx", None),
        P("dp", "ctx", None),
        P("dp", "ctx", None),
        P("dp", None),
        P("dp", None),
        P("dp"),
    )
    return jax.shard_map(
        functools.partial(per_device, mesh.shape["ctx"], mesh.shape["dp"]),
        mesh=mesh,
        in_specs=placed,
        out_specs=(P("dp", None), P("dp", "ctx", None), P("dp", "ctx", None), P("dp", "ctx", None)),
        check_vma=False,
    )
```

time: 220 us -> 52.6 us (0.24)
  waiting for transfers between devices: 104 us -> 0 us
  blocking collectives: 55.8 us -> 0 us
  Pallas kernels: 0 us -> 45.1 us
  matrix products: 19.6 us -> 0 us
  between operations: 17.3 us -> 0.66 us
  local copies, waits for them, and re-layouts: 14.8 us -> 5.96 us
  other arithmetic: 7.26 us -> 0 us
    unnamed x4 -> x0, waiting for transfers between devices: 68.4 us -> none
    pallas_call x0 -> x1, Pallas kernels: none -> 45.1 us  [per_device(): pl.pallas_call(functools.partial(kernel, n_ctx, n_dp), out_shape=(jax.Sha...]
    all_gather x3 -> x0, blocking collectives: 44.1 us -> none  [the longest x1 31 us: per_device(): lax.all_gather(document_normalized, 'dp', axis=0, tiled=True)]
    reduce_scatter x2 -> x0, waiting for transfers between devices: 36 us -> none  [the longest x1 23.1 us: per_device(): lax.psum_scatter(value_terms.reshape(1, seq_len, kv_width).astype(jnp.bfl...]
    dot_general x12 -> x0, matrix products: 19.6 us -> none  [the longest x1 3.18 us: back_step(): jnp.einsum('tgqd,sgd->gqts', out_heads, v_rows, preferred_element_type=jn...]
    psum x1 -> x0, blocking collectives: 11.6 us -> none  [per_device(): lax.psum(jnp.dot(member, attended, precision=FULL_ACCURACY), 'ctx')]
    convert_element_type x5 -> x0, local copies, waits for them, and re-layouts: 5.45 us -> none  [the longest x2 2.09 us: per_device(): key_terms.reshape(1, seq_len, kv_width).astype(jnp.bfloat16)]
    reduce_sum x8 -> x0, other arithmetic: 3.69 us -> none  [the longest x1 1.33 us: per_device(): doc_begin = jnp.sum(jnp.where(doc_index == query_doc[0], doc_starts, 0))]
  transfers between devices with their start and end apart: 3 -> 0, of which waited for: 3 -> 0; matrix products, arithmetic and copies ran while one was open for 4% -> 0% of each run, Pallas kernels for 0% -> 0%
where the time goes in v1:
time: 52.6 us; the launch traced here: 51.7 us
  Pallas kernels  45.1 us (86%)
  local copies, waits for them, and re-layouts  5.96 us (11%)
  between operations  0.66 us (1%)
    pallas_call x1, Pallas kernels, per_device(): pl.pallas_call(functools.partial(kernel, n_ctx, n_dp), out_shape=(jax.Sha...  45.1 us
    unnamed x12, local copies, waits for them, and re-layouts  5.22 us

profile of v1, /device:TPU:0, one launch (start us, length us, event | category | flops | bytes accessed | tf_op | source)
XLA Modules:
  0.0 51.7 jit_solution(6433261174522711769)
XLA Ops:
  0.6 0.0 copy-start.3
  0.6 0.6 %copy-done.3 = s32[128]{0:T(128)S(1)} copy-done((s32[128]{0:T(128)S(1)}, s32[128]{0:T(128)}, u32[]{:S(2)}) %copy-start.3) | copy-done | bytes 536
  1.3 0.7 %copy.10.pos_ref = s32[128,1]{1,0:T(8,128)} copy(s32[128,1]{0,1:T(1,128)S(1)} %bitcast.1) | data formatting | bytes 1024 | tf_op jit(solution)/shard_map/broadcast_in_dim | solution.py:352
  2.0 45.1 %shard_map.93 = (f32[128,1792]{1,0:T(8,128)}, bf16[1,128,1792]{2,1,0:T(8,128)(2,1)}, bf16[1,128,256]{2,1,0:T(8,128)(2,1)}, bf16[1,128,256]{2,1,0:T(8,128)(2,1)}) custom-call(s32[1,4]{1,0:T(1,128)} %len_ref.1, bf16[1,128,1792]{2,1,0:T(8,128)(2,1)} %q_ref.1, bf16[1,128,256]{2,1,0:T(8,128)(2,1)} %k_ref.1, bf16[1,128,256]{2,1,0:T(8,128)(2,1)} %v_ref.1, ...), custom_call_target="tpu_custom_call" | custom-call | tf_op jit(solution)/shard_map/pallas_call | solution.py:313
  47.2 0.0 copy-start
  47.2 2.2 %copy.15 = f32[128,1792]{1,0:T(8,128)} copy(f32[128,1792]{1,0:T(8,128)} %get-tuple-element.8) | data formatting | bytes 1835008
  49.4 0.0 copy-done
  49.4 0.0 copy-start.2
  49.4 0.8 %copy.16 = bf16[1,128,1792]{2,1,0:T(8,128)(2,1)} copy(bf16[1,128,1792]{2,1,0:T(8,128)(2,1)S(1)} %copy-done) | data formatting | bytes 917504
  50.1 0.1 copy-done.2
  50.2 0.0 copy-start.1
  50.2 0.6 %copy.17 = bf16[1,128,256]{2,1,0:T(8,128)(2,1)} copy(bf16[1,128,256]{2,1,0:T(8,128)(2,1)S(1)} %copy-done.2) | data formatting | bytes 131072
  50.9 0.2 copy-done.1
  51.1 0.6 %copy.18 = bf16[1,128,256]{2,1,0:T(8,128)(2,1)} copy(bf16[1,128,256]{2,1,0:T(8,128)(2,1)S(1)} %copy-done.1) | data formatting | bytes 131072
Async XLA Ops:
  0.6 0.7 %copy-start.3 = (s32[128]{0:T(128)S(1)}, s32[128]{0:T(128)}, u32[]{:S(2)}) copy-start(s32[128]{0:T(128)} %param.11) | copy-start | bytes 1540
  47.2 2.2 %copy-start = (bf16[1,128,1792]{2,1,0:T(8,128)(2,1)S(1)}, bf16[1,128,1792]{2,1,0:T(8,128)(2,1)}, u32[]{:S(2)}) copy-start(bf16[1,128,1792]{2,1,0:T(8,128)(2,1)} %get-tuple-element.9) | copy-start | bytes 1376260
  49.4 0.9 %copy-start.2 = (bf16[1,128,256]{2,1,0:T(8,128)(2,1)S(1)}, bf16[1,128,256]{2,1,0:T(8,128)(2,1)}, u32[]{:S(2)}) copy-start(bf16[1,128,256]{2,1,0:T(8,128)(2,1)} %get-tuple-element.10) | copy-start | bytes 196612
  50.2 0.9 %copy-start.1 = (bf16[1,128,256]{2,1,0:T(8,128)(2,1)S(1)}, bf16[1,128,256]{2,1,0:T(8,128)(2,1)}, u32[]{:S(2)}) copy-start(bf16[1,128,256]{2,1,0:T(8,128)(2,1)} %get-tuple-element.11) | copy-start | bytes 196612

commit v2 on v1

--- a/solution.py
+++ b/solution.py
@@ -53,9 +53,9 @@
     len_ref, q_ref, k_ref, v_ref, emb_ref, pos_ref,
     qg_ref, gq_ref, gk_ref, gv_ref,
     k_all, v_all, q_s, probs, att, bias, sums, units, terms, doc_hi, doc_lo,
-    doc_grad, out_low, s_grad, weights, k_out, v_out, k_in, v_in,
-    kv_send, kv_recv, sum_send, sum_recv, unit_send, unit_recv, term_send, term_recv,
-    part_send, part_recv,
+    doc_grad, col_sums, flows, s_grad, k_out, v_out, k_in, v_in, pair,
+    kv_send, kv_recv, sum_send, sum_recv, unit_send, unit_recv, unit_relay, term_send, term_recv,
+    pair_send, pair_recv, part_send, part_recv,
 ):
     me = lax.axis_index("ctx")
     row = lax.axis_index("dp")
@@ -64,13 +64,22 @@
     emb = q_ref.shape[2]
     half = emb // 2
     factor = HEAD_DIM ** (-0.5)
-    sibling = me + 1 - 2 * lax.rem(me, 2)
+    core = lax.rem(me, 2)
+    sibling = me + 1 - 2 * core
 
     def ctx_peer(t):
         return lax.rem(me + t, n_ctx)
 
     def dp_peer(t):
         return lax.rem(row + t, n_dp)
+
+    def each_row(parity, action):
+        for u in range(n_dp // 2):
+            t = 2 * u + 1 + parity
+            if 2 * u + 2 < n_dp:
+                action(u, t)
+            else:
+                pl.when(parity == 0)(functools.partial(action, u, t))
 
     def block(ref, idx):
         return ref.at[pl.ds(pl.multiple_of(idx * tok, tok), tok)]
@@ -91,6 +100,7 @@
         )
         copy.start()
         started.append(copy)
+        return copy
 
     def arrive(dst, send_sem, recv_sem, device):
         pltpu.make_async_remote_copy(
@@ -134,8 +144,21 @@
     doc_len = jnp.zeros((WIRE, 1), F32)
     for d in range(DOCS):
         doc_len = jnp.where(len_doc == d, len_ref[0, d].astype(F32), doc_len)
+    k_mask = (
+        doc_at(lax.broadcasted_iota(jnp.int32, (WIRE, seq), 1))
+        == lax.rem(lax.broadcasted_iota(jnp.int32, (WIRE, seq), 0), DOCS)
+    ).astype(F32)
+    low_keys = lax.broadcasted_iota(jnp.int32, (WIRE, seq), 0) < DOCS
+    col_sums[PER_GROUP * WIRE:, :] = jnp.zeros((WIRE, seq), F32)
     for h in range(HEADS):
         q_s[h * tok:(h + 1) * tok, :] = q_ref[0, :, h * HEAD_DIM:(h + 1) * HEAD_DIM]
+    nq = emb_ref.shape[0]
+    diagonal = lax.broadcasted_iota(jnp.int32, (nq, nq), 0) == lax.broadcasted_iota(
+        jnp.int32, (nq, nq), 1
+    )
+    positive = jnp.sum(
+        jnp.where(diagonal, pos_ref[...].astype(F32), 0.0), axis=1, keepdims=True
+    ).astype(jnp.int32)
     q_sq = jnp.zeros((emb_ref.shape[0], HEAD_DIM), F32)
     for h in range(HEADS):
         part = emb_ref[:, h * HEAD_DIM:(h + 1) * HEAD_DIM].astype(F32)
@@ -159,7 +182,7 @@
         return pl.ds(pl.multiple_of((g * PER_GROUP + i) * tok, tok), tok)
 
     def forward(i, carry):
-        docs = []
+        docs, cols_of = [], []
         for g in range(KV_HEADS):
             rows = head_rows(g, i)
             k_g = k_all[:, g * HEAD_DIM:(g + 1) * HEAD_DIM]
@@ -168,15 +191,19 @@
             e = jnp.exp(scores - jnp.max(scores, axis=1, keepdims=True))
             p = e * (1.0 / jnp.sum(e, axis=1, keepdims=True))
             probs[rows, :] = p
-            out = dot_nn(p.astype(BF16), v_g)
+            low = p.astype(BF16)
+            cols_of.append(jnp.sum(low.astype(F32), axis=0, keepdims=True))
+            out = dot_nn(low, v_g)
             att[rows, :] = out
-            high, low = split(out)
-            docs.append(dot_nn(member, high) + dot_nn(member, low))
+            out_hi, out_lo = split(out)
+            docs.append(dot_nn(member, out_hi) + dot_nn(member, out_lo))
+        wire_rows = pl.ds(pl.multiple_of(i * WIRE, WIRE), WIRE)
+        col_sums[wire_rows, :] = jnp.where(low_keys, cols_of[0], cols_of[1]) * k_mask
         cols = pl.ds(pl.multiple_of(i * HEAD_DIM, HEAD_DIM), HEAD_DIM)
         sums[me, :, cols] = jnp.where(low_rows, docs[0], docs[1])
         return carry
 
-    lax.fori_loop(0, PER_GROUP, forward, 0)
+    lax.fori_loop(0, PER_GROUP, forward, 0, unroll=True)
     for t in range(1, n_ctx):
         send(sums.at[me], sums.at[me], sum_send.at[t], sum_recv.at[me], {"ctx": ctx_peer(t)})
     for t in range(1, n_ctx):
@@ -189,11 +216,30 @@
     doc_inv = lax.rsqrt(doc_row_sum(doc_emb * doc_emb) + EPSILON)
     doc_unit = doc_emb * doc_inv
     units[row] = doc_unit
-    for t in range(1, n_dp):
-        send(units.at[row], units.at[row], unit_send.at[t], unit_recv.at[row], {"dp": dp_peer(t)})
-    for t in range(1, n_dp):
-        idx = dp_peer(t)
-        arrive(units.at[idx], unit_send.at[t], unit_recv.at[idx], {"dp": idx})
+    def send_unit(u, t):
+        send(units.at[row], units.at[row], unit_send.at[u], unit_recv.at[row], {"dp": dp_peer(t)})
+
+    def relay_unit(u, t):
+        idx = dp_peer(n_dp - t)
+        arrive(units.at[idx], unit_send.at[u], unit_recv.at[idx], {"dp": idx})
+        send(units.at[idx], units.at[idx], unit_relay.at[u], unit_recv.at[idx], {"ctx": sibling})
+
+    def take_unit(u, t):
+        idx = dp_peer(n_dp - t)
+        arrive(units.at[idx], unit_relay.at[u], unit_recv.at[idx], {"ctx": sibling})
+
+    def sent_unit(u, t):
+        for sem in (unit_send.at[u], unit_relay.at[u]):
+            pltpu.make_async_remote_copy(
+                src_ref=units.at[row], dst_ref=units.at[row], send_sem=sem,
+                recv_sem=unit_recv.at[row], device_id={"ctx": sibling}, device_id_type=MESH,
+            ).wait_send()
+
+    kept = len(started)
+    each_row(core, send_unit)
+    each_row(core, relay_unit)
+    each_row(1 - core, take_unit)
+    del started[kept:]
 
     low_half = lax.broadcasted_iota(jnp.int32, (WIRE, half), 0) < DOCS
     for r in range(0, n_dp, 2):
@@ -214,7 +260,7 @@
     once = lax.rem(column, WIRE) < DOCS
     doc_of = (column // WIRE) * DOCS + lax.rem(column, DOCS)
     e = jnp.exp(logits)
-    target = (doc_of == pos_ref[...]).astype(F32)
+    target = (doc_of == positive).astype(F32)
     coef = e / jnp.sum(jnp.where(once, e, 0.0), axis=1, keepdims=True) - target
 
     c_hi, c_lo = split(coef * (q_inv * SCALE_UP))
@@ -227,10 +273,24 @@
                 terms[1, r] = rows
             else:
                 terms[1, r] = jnp.where(low_half, terms[1, r], rows)
-    for t in range(1, n_dp):
+    def send_term(u, t):
         idx = dp_peer(t)
-        send(terms.at[1, idx], terms.at[0, row], term_send.at[t], term_recv.at[row], {"dp": idx})
-    terms[0, row] = terms[1, row]
+        send(terms.at[1, idx], terms.at[0, row], term_send.at[u], term_recv.at[row], {"dp": idx})
+
+    def take_term(u, t):
+        idx = dp_peer(n_dp - t)
+        arrive(terms.at[0, idx], term_send.at[u], term_recv.at[idx], {"dp": idx})
+        pair[core] += terms[0, idx]
+
+    def sent_term(u, t):
+        pltpu.make_async_remote_copy(
+            src_ref=terms.at[1, row], dst_ref=terms.at[0, row], send_sem=term_send.at[u],
+            recv_sem=term_recv.at[row], device_id={"ctx": sibling}, device_id_type=MESH,
+        ).wait_send()
+
+    kept = len(started)
+    each_row(core, send_term)
+    del started[kept:]
 
     coef_once = jnp.where(once, coef, 0.0)
     inner = jnp.sum(coef_once * logits, axis=1, keepdims=True) * q_inv
@@ -241,45 +301,53 @@
         u = dot_nn(c_hi, d_hi) + dot_nn(c_lo, d_hi) + dot_nn(c_hi, doc_lo[:, at:at + step])
         qg_ref[:, at:at + step] = q_inv * (u - emb_ref[:, at:at + step].astype(F32) * inner)
 
-    for t in range(1, n_dp):
-        idx = dp_peer(t)
-        arrive(terms.at[0, idx], term_send.at[t], term_recv.at[idx], {"dp": idx})
-    w = terms[0, 0]
-    for r in range(1, n_dp):
-        w = w + terms[0, r]
+    pair[core] = jnp.zeros((WIRE, half), F32)
+    each_row(core, take_term)
+    send(pair.at[core], pair.at[core], pair_send, pair_recv, {"ctx": sibling})
+    arrive(pair.at[1 - core], pair_send, pair_recv, {"ctx": sibling})
+    w = terms[1, row] + (pair[0] + pair[1])
     doc_grad[...] = doc_inv * (w - doc_unit * doc_row_sum(doc_unit * w)) / doc_len
 
-    def backward(i, carry):
-        cols = pl.ds(pl.multiple_of(i * HEAD_DIM, HEAD_DIM), HEAD_DIM)
-        for g in range(KV_HEADS):
-            rows = head_rows(g, i)
-            og = jnp.zeros((tok, HEAD_DIM), F32)
-            grads = doc_grad[:, cols]
-            for d in range(DOCS):
-                og = jnp.where(doc_col == d, grads[g * DOCS + d:g * DOCS + d + 1], og)
-            delta = jnp.sum(og * att[rows, :], axis=1, keepdims=True)
-            low = og.astype(BF16)
-            out_low[rows, :] = low
-            flow = dot_nt(low, v_all[:, g * HEAD_DIM:(g + 1) * HEAD_DIM])
-            p = probs[rows, :]
-            weights[rows, :] = p.astype(BF16)
-            s_grad[rows, :] = (p * (flow - delta)).astype(BF16)
-        return carry
-
-    lax.fori_loop(0, PER_GROUP, backward, 0)
-
-    span = PER_GROUP * tok
-    for a, lhs, rhs, out, into, scale in (
-        (0, weights, out_low, v_out, v_in, 1.0),
-        (1, s_grad, q_s, k_out, k_in, factor),
-    ):
-        for g in range(KV_HEADS):
-            part = dot_tn(lhs[g * span:(g + 1) * span, :], rhs[g * span:(g + 1) * span, :])
-            out[:, g * HEAD_DIM:(g + 1) * HEAD_DIM] = (part * scale).astype(BF16)
+    def send_parts(a, out, into):
         for t in range(1, n_ctx):
             idx = ctx_peer(t)
             send(block(out, idx), into.at[me], part_send.at[a, t], part_recv.at[a, me], {"ctx": idx})
         into[me] = out[pl.ds(pl.multiple_of(me * tok, tok), tok), :]
+
+    low = jnp.concatenate(
+        [doc_grad[:, i * HEAD_DIM:(i + 1) * HEAD_DIM] for i in range(PER_GROUP)]
+        + [jnp.zeros((WIRE, HEAD_DIM), F32)], axis=0
+    )
+    low_docs = lax.rem(lax.broadcasted_iota(jnp.int32, low.shape, 0), WIRE) < DOCS
+    low_parts = jnp.concatenate(
+        [jnp.where(low_docs, low, 0.0), jnp.where(low_docs, 0.0, low)], axis=1
+    ).astype(BF16)
+    s_hi, s_lo = split(col_sums[...])
+    v_out[...] = (dot_tn(s_hi, low_parts) + dot_tn(s_lo, low_parts)).astype(BF16)
+    send_parts(0, v_out, v_in)
+    flows[...] = dot_nt(low_parts, v_all[...])
+
+    def backward(i, carry):
+        cols = pl.ds(pl.multiple_of(i * HEAD_DIM, HEAD_DIM), HEAD_DIM)
+        grads = doc_grad[:, cols]
+        flow_rows = flows[pl.ds(pl.multiple_of(i * WIRE, WIRE), WIRE), :] * k_mask
+        for g in range(KV_HEADS):
+            rows = head_rows(g, i)
+            og = jnp.zeros((tok, HEAD_DIM), F32)
+            for d in range(DOCS):
+                og = jnp.where(doc_col == d, grads[g * DOCS + d:g * DOCS + d + 1], og)
+            delta = jnp.sum(og * att[rows, :], axis=1, keepdims=True)
+            flow = jnp.sum(flow_rows[g * DOCS:(g + 1) * DOCS], axis=0, keepdims=True)
+            s_grad[rows, :] = (probs[rows, :] * (flow - delta)).astype(BF16)
+        return carry
+
+    lax.fori_loop(0, PER_GROUP, backward, 0, unroll=True)
+
+    span = PER_GROUP * tok
+    for g in range(KV_HEADS):
+        part = dot_tn(s_grad[g * span:(g + 1) * span, :], q_s[g * span:(g + 1) * span, :])
+        k_out[:, g * HEAD_DIM:(g + 1) * HEAD_DIM] = (part * factor).astype(BF16)
+    send_parts(1, k_out, k_in)
 
     for g in range(KV_HEADS):
         k_g = k_all[:, g * HEAD_DIM:(g + 1) * HEAD_DIM]
@@ -299,6 +367,8 @@
 
     for copy in started:
         copy.wait_send()
+    each_row(core, sent_unit)
+    each_row(core, sent_term)
 
 
 def per_device(n_ctx, n_dp, queries_q, keys, values, lengths, query_emb, positive):
@@ -333,23 +403,25 @@
             pltpu.VMEM((n_dp * WIRE, emb), BF16),
             pltpu.VMEM((n_dp * WIRE, emb), BF16),
             pltpu.VMEM((WIRE, half), F32),
-            pltpu.VMEM((n_rows, HEAD_DIM), BF16),
-            pltpu.VMEM((n_rows, seq), BF16),
+            pltpu.VMEM(((PER_GROUP + 1) * WIRE, seq), F32),
+            pltpu.VMEM(((PER_GROUP + 1) * WIRE, seq), F32),
             pltpu.VMEM((n_rows, seq), BF16),
             pltpu.VMEM((seq, kv_width), BF16),
             pltpu.VMEM((seq, kv_width), BF16),
             pltpu.VMEM((n_ctx, tok, kv_width), BF16),
             pltpu.VMEM((n_ctx, tok, kv_width), BF16),
+            pltpu.VMEM((2, WIRE, half), F32),
             dma((2, n_ctx)), dma((2, n_ctx)),
             dma((n_ctx,)), dma((n_ctx,)),
-            dma((n_dp,)), dma((n_dp,)),
-            dma((n_dp,)), dma((n_dp,)),
+            dma((n_dp // 2,)), dma((n_dp,)), dma((n_dp // 2,)),
+            dma((n_dp // 2,)), dma((n_dp,)),
+            dma(()), dma(()),
             dma((2, n_ctx)), dma((2, n_ctx)),
         ],
         compiler_params=pltpu.CompilerParams(
             collective_id=0, has_side_effects=True, vmem_limit_bytes=56 * 1024 * 1024
         ),
-    )(lengths, queries_q, keys, values, query_emb, positive[:, None])
+    )(lengths, queries_q, keys, values, query_emb, positive[None, :])
 
 
 def solution(mesh):

time: 52.6 us -> 49.3 us (0.937)
  Pallas kernels: 45.1 us -> 43.2 us
  local copies, waits for them, and re-layouts: 5.96 us -> 4.57 us
    pallas_call x1, Pallas kernels: 45.1 us -> 43.2 us  [per_device(): pl.pallas_call(functools.partial(kernel, n_ctx, n_dp), out_shape=(jax.Sha...]
    broadcast_in_dim x1 -> x0, local copies, waits for them, and re-layouts: 0.74 us -> none  [per_device(): positive[:, None]]
    unnamed x12 -> x10, local copies, waits for them, and re-layouts: 5.22 us -> 4.57 us
where the time goes in v2:
time: 49.3 us; the launch traced here: 48.4 us
  Pallas kernels  43.2 us (88%)
  local copies, waits for them, and re-layouts  4.57 us (9%)
  between operations  0.65 us (1%)
    pallas_call x1, Pallas kernels, per_device(): pl.pallas_call(functools.partial(kernel, n_ctx, n_dp), out_shape=(jax.Sha...  43.2 us
    unnamed x10, local copies, waits for them, and re-layouts  4.57 us

profile of v2, /device:TPU:0, one launch (start us, length us, event | category | flops | bytes accessed | tf_op | source)
XLA Modules:
  0.0 48.4 jit_solution(5683823625042782692)
XLA Ops:
  0.6 43.2 %shard_map.93 = (f32[128,1792]{1,0:T(8,128)}, bf16[1,128,1792]{2,1,0:T(8,128)(2,1)}, bf16[1,128,256]{2,1,0:T(8,128)(2,1)}, bf16[1,128,256]{2,1,0:T(8,128)(2,1)}) custom-call(s32[1,4]{1,0:T(1,128)} %len_ref.1, bf16[1,128,1792]{2,1,0:T(8,128)(2,1)} %q_ref.1, bf16[1,128,256]{2,1,0:T(8,128)(2,1)} %k_ref.1, bf16[1,128,256]{2,1,0:T(8,128)(2,1)} %v_ref.1, ...), custom_call_target="tpu_custom_call" | custom-call | tf_op jit(solution)/shard_map/pallas_call | solution.py:383
  43.9 0.0 copy-start
  43.9 2.2 %copy.14 = f32[128,1792]{1,0:T(8,128)} copy(f32[128,1792]{1,0:T(8,128)} %get-tuple-element.8) | data formatting | bytes 1835008
  46.1 0.0 copy-done
  46.1 0.0 copy-start.2
  46.1 0.8 %copy.15 = bf16[1,128,1792]{2,1,0:T(8,128)(2,1)} copy(bf16[1,128,1792]{2,1,0:T(8,128)(2,1)S(1)} %copy-done) | data formatting | bytes 917504
  46.9 0.1 copy-done.2
  46.9 0.0 copy-start.1
  46.9 0.6 %copy.16 = bf16[1,128,256]{2,1,0:T(8,128)(2,1)} copy(bf16[1,128,256]{2,1,0:T(8,128)(2,1)S(1)} %copy-done.2) | data formatting | bytes 131072
  47.6 0.2 copy-done.1
  47.8 0.6 %copy.17 = bf16[1,128,256]{2,1,0:T(8,128)(2,1)} copy(bf16[1,128,256]{2,1,0:T(8,128)(2,1)S(1)} %copy-done.1) | data formatting | bytes 131072
Async XLA Ops:
  43.9 2.2 %copy-start = (bf16[1,128,1792]{2,1,0:T(8,128)(2,1)S(1)}, bf16[1,128,1792]{2,1,0:T(8,128)(2,1)}, u32[]{:S(2)}) copy-start(bf16[1,128,1792]{2,1,0:T(8,128)(2,1)} %get-tuple-element.9) | copy-start | bytes 1376260
  46.1 0.9 %copy-start.2 = (bf16[1,128,256]{2,1,0:T(8,128)(2,1)S(1)}, bf16[1,128,256]{2,1,0:T(8,128)(2,1)}, u32[]{:S(2)}) copy-start(bf16[1,128,256]{2,1,0:T(8,128)(2,1)} %get-tuple-element.10) | copy-start | bytes 196612
  46.9 0.9 %copy-start.1 = (bf16[1,128,256]{2,1,0:T(8,128)(2,1)S(1)}, bf16[1,128,256]{2,1,0:T(8,128)(2,1)}, u32[]{:S(2)}) copy-start(bf16[1,128,256]{2,1,0:T(8,128)(2,1)} %get-tuple-element.11) | copy-start | bytes 196612
